TPU v7x, 128 devices: a whole 4x4x4 slice. The times are simulated.
128 devices in a mesh: dp: 16 (over x, y_lo, core), row: 4 (over z), col: 2 (over y_hi).
Axes of the slice: x: 4, y: 4 (y_hi: 2, y_lo: 2; y = y_hi * 2 + y_lo), z: 4, core: 2. Of those that a mesh axis runs over, the one named last changes fastest.
Arguments:
- activations: bfloat16 [16384, 896], P('dp', 'row'), may hold values from -6 to 6
- starts: int32 [16384], P('dp'), may hold values from 0 to 16383, as said below
- first_gain: float32 [896], P('row'), may hold values from 0.5 to 1.5
- project_weight: bfloat16 [896, 1152], P('row', 'col'), may hold values from -0.1875 to 0.1875
- project_bias: float32 [1152], P('col'), may hold values from -3 to 3
- output_weight: bfloat16 [896, 896], P('col', 'row'), may hold values from -0.75 to 0.75
- second_gain: float32 [896], P('row'), may hold values from 0.5 to 1.5
- gate_weight: bfloat16 [896, 4864], P('row', 'col'), may hold values from -0.1875 to 0.1875
- up_weight: bfloat16 [896, 4864], P('row', 'col'), may hold values from -0.1875 to 0.1875
- down_weight: bfloat16 [4864, 896], P('col', 'row'), may hold values from -0.15625 to 0.15625
- cotangent: bfloat16 [16384, 896], P('dp', 'row'), may hold values from -6 to 6
Outputs:
- block_output: bfloat16 [16384, 896], P('dp', 'row')
- input_grad: float32 [16384, 896], P('dp', 'row')
- first_gain_grad: float32 [896], P('row')
- project_weight_grad: float32 [896, 1152], P('row', 'col')
- project_bias_grad: float32 [1152], P('col')
- output_weight_grad: float32 [896, 896], P('col', 'row')
- second_gain_grad: float32 [896], P('row')
- gate_weight_grad: float32 [896, 4864], P('row', 'col')
- up_weight_grad: float32 [896, 4864], P('row', 'col')
- down_weight_grad: float32 [4864, 896], P('col', 'row')
Inputs may be any that keep to these rules, and one draw needn't show every extreme that they name: starts never falls, starts[t] <= t, and starts[t] is t or starts[t - 1]; a sequence holds at most 1024 tokens, and one holds exactly 1024.
All inputs are finite; a program needn't handle non-finite values.
Results may differ from a plain program's by a relative error of at most 0.012.
Values may be sent and summed in bfloat16 or wider, within the bound.
A program may use at most 192 MiB of HBM per device.

v0:
```python
import functools

import jax
import jax.numpy as jnp
from jax import lax
from jax.experimental import pallas as pl
from jax.experimental.pallas import tpu as pltpu
from jax.sharding import PartitionSpec as P

D = 896
HEADS = 14
GROUPS = 2
HEAD_DIM = 64
MAXLEN = 1024
EPS = 1e-06
BF = jnp.bfloat16
F32 = jnp.float32
ROWS = 4
FEAT = 224
SHARE = 256
SHARD = 1024
HALF_FF = 2432
WIN = 640
LAST = HALF_FF - WIN
PADF = 256
VMEM_LIMIT = 60 * 1024 * 1024


def dot(a, b):
    return jnp.dot(a, b, preferred_element_type=F32)


def dot_nt(a, b):
    return lax.dot_general(a, b, (((1,), (1,)), ((), ())), preferred_element_type=F32)


def dot_tn(a, b):
    return lax.dot_general(a, b, (((0,), (0,)), ((), ())), preferred_element_type=F32)


def rcopy(src, dst, send, recv, **device):
    return pltpu.make_async_remote_copy(
        src_ref=src,
        dst_ref=dst,
        send_sem=send,
        recv_sem=recv,
        device_id=device,
        device_id_type=pl.DeviceIdType.MESH,
    )


def greet(peers):
    barrier = pltpu.get_barrier_semaphore()
    for peer in peers:
        pl.semaphore_signal(
            barrier, inc=1, device_id=peer, device_id_type=pl.DeviceIdType.MESH
        )
    pl.semaphore_wait(barrier, len(peers))


def vmem_call(kernel, inputs, outs, scratch, collective, cost=None):
    return pl.pallas_call(
        kernel,
        out_shape=outs,
        in_specs=[pl.BlockSpec(memory_space=pltpu.VMEM)] * inputs,
        out_specs=jax.tree.map(lambda _: pl.BlockSpec(memory_space=pltpu.VMEM), outs),
        scratch_shapes=scratch,
        compiler_params=pltpu.CompilerParams(
            collective_id=collective,
            has_side_effects=True,
            vmem_limit_bytes=VMEM_LIMIT,
        ),
        cost_estimate=cost,
    )


def swapped(values):
    width = values.shape[1]
    lane = lax.broadcasted_iota(jnp.int32, values.shape, 1)
    return jnp.where(
        lax.rem(lane, 64) < 32,
        pltpu.roll(values, width - 32, 1),
        pltpu.roll(values, 32, 1),
    )


def forward_kernel(
    act_ref,
    cot_ref,
    proj_ref,
    outw_ref,
    gate_ref,
    up_ref,
    down_ref,
    gains_ref,
    bias_ref,
    cos_ref,
    sin_ref,
    start_ref,
    x_out,
    nf_out,
    q_out,
    kv_out,
    lse_out,
    att_out,
    mid_out,
    proj_full,
    outw_full,
    gains_full,
    cot_out,
    second_out,
    op_out,
    grads_out,
    gate_full,
    up_full,
    down_full,
    cot_all,
    mask,
    own_kv,
    c_send,
    c_in,
    second_in,
    ns_all,
    hid,
    gg,
    gu,
    sp_send,
    sp_in,
    sem_x,
    sem_g,
    sem_w,
    sem_wx,
    sem_wc,
    sem_cot,
    sem_kv,
    sem_c,
    sem_ag,
    sem_sp,
    sem_cs,
    sem_l,
):
    d = lax.axis_index("dp")
    r = lax.axis_index("row")
    c = lax.axis_index("col")
    core = lax.rem(d, 2)
    x_at = d // 4
    sibling = d + 1 - 2 * core
    x_peers = [(k, lax.rem(x_at + k, 4) * 4 + lax.rem(d, 4)) for k in (1, 2, 3)]
    block = 4 * d + r
    near = lambda i: {
        "dp": lax.rem((block + 64 + i) // 4, 16),
        "row": lax.rem(r + 4 + i, 4),
    }
    greet(
        [{"row": lax.rem(r + k, 4)} for k in (1, 2, 3)]
        + [{"dp": p} for _, p in x_peers]
        + [{"col": 1 - c}, {"dp": sibling}]
        + [near(i) for i in (1, 2, 3, 4, -1, -2, -3, -4)]
    )
    pending = []

    def go(*args, **device):
        copy = rcopy(*args, **device)
        copy.start()
        pending.append(copy)
        return copy

    peers = [(k, lax.rem(r + k, 4)) for k in (1, 2, 3)]
    span = lambda q: pl.ds(pl.multiple_of(q * SHARE, SHARE), SHARE)
    offset = lambda q: pl.multiple_of(jnp.minimum(q * WIN, LAST), 128)
    half = lambda n: pl.ds(pl.multiple_of(core * n, 16), n)

    def down_rows(q):
        return pl.ds(pl.multiple_of(offset(q) + core * (WIN // 2), 16), WIN // 2)

    pieces = (
        (lambda q: proj_ref.at[half(112), :], proj_full, 112),
        (lambda q: outw_ref.at[half(224), :], outw_full, 224),
        (lambda q: gate_ref.at[half(112), pl.ds(offset(q), WIN)], gate_full, 112),
        (lambda q: up_ref.at[half(112), pl.ds(offset(q), WIN)], up_full, 112),
        (lambda q: down_ref.at[down_rows(q), :], down_full, WIN // 2),
    )

    def crossing(w):
        source, full, n = pieces[w]
        return [
            rcopy(
                source(q),
                full.at[r, half(n), :],
                sem_w.at[0, w, k - 1],
                sem_w.at[1, w, k - 1],
                row=q,
            )
            for k, q in peers
        ]

    def passing(w):
        _, full, n = pieces[w]
        copies = []
        for k, q in peers:
            part = full.at[q, half(n), :]
            for e, device in x_peers:
                copies.append(
                    rcopy(
                        part,
                        part,
                        sem_wx.at[0, w - 2, k - 1, e - 1],
                        sem_wx.at[1, w - 2, k - 1, 0],
                        dp=device,
                    )
                )
        return copies

    def fetch(w):
        source, full, n = pieces[w]
        local = pltpu.make_async_copy(source(r), full.at[r, half(n), :], sem_l.at[w])
        local.start()
        copies = crossing(w)
        if w < 2:
            for copy in copies:
                copy.start()
                pending.append(copy)
        else:

            @pl.when(x_at == w - 2)
            def _():
                for copy in copies:
                    copy.start()

        return copies, local

    def pass_on(w, fetched):
        @pl.when(x_at == w - 2)
        def _():
            for copy in fetched[0]:
                copy.wait_recv()
            for copy in passing(w):
                copy.start()

    def share(w, fetched):
        _, full, n = pieces[w]
        copies, local = fetched
        local.wait()
        if w < 2:
            for copy in copies:
                copy.wait_recv()
        else:

            @pl.when(x_at != w - 2)
            def _():
                for copy in passing(w)[::3]:
                    copy.wait_recv()

        part = full.at[:, half(n), :]
        copy = rcopy(part, part, sem_wc.at[0, w], sem_wc.at[1, w], dp=sibling)
        copy.start()
        if w < 2:
            pending.append(copy)
        return copy

    def finish(w, fetched):
        @pl.when(x_at == w - 2)
        def _():
            for copy in fetched[0] + passing(w):
                copy.wait_send()

    x_copies = [
        go(
            act_ref.at[span(q), :],
            x_out.at[r],
            sem_x.at[0, k - 1],
            sem_x.at[1, k - 1],
            row=q,
        )
        for k, q in peers
    ]
    g_copies = [
        go(gains_ref, gains_full.at[r], sem_g.at[0, k - 1], sem_g.at[1, k - 1], row=q)
        for k, q in peers
    ]
    fetched = {0: fetch(0)}
    x_out[r] = act_ref[span(r), :]
    gains_full[r] = gains_ref[...]
    query_at = lax.broadcasted_iota(jnp.int32, (SHARE, 1), 0) + MAXLEN
    key_at = lax.broadcasted_iota(jnp.int32, (SHARE, MAXLEN + SHARE), 1)
    mask[...] = jnp.where(
        (key_at >= start_ref[...]) & (key_at <= query_at), 0.0, -1e30
    )
    shared = {0: share(0, fetched[0])}
    for copy in x_copies + g_copies:
        copy.wait_recv()
    for w in (1, 2, 3, 4):
        fetched[w] = fetch(w)
    cot_all[r] = cot_ref[...]
    square = jnp.zeros((SHARE, 1), F32)
    for j in range(4):
        value = x_out[j].astype(F32)
        square += jnp.sum(value * value, axis=1, keepdims=True)
    rate = lax.rsqrt(square / D + EPS)
    for j in range(4):
        nf_out[j] = (x_out[j].astype(F32) * rate * gains_full[j, 0:1, :]).astype(BF)
    shared[0].wait_recv()
    projected = dot(nf_out[0], proj_full[0, :, 0:512])
    values = dot(nf_out[0], proj_full[0, :, 512:576])
    for j in range(1, 4):
        projected += dot(nf_out[j], proj_full[j, :, 0:512])
        values += dot(nf_out[j], proj_full[j, :, 512:576])
    projected += bias_ref[:, 0:512]
    values = (values + bias_ref[:, 512:576]).astype(BF)
    cosine = jnp.concatenate([cos_ref[...]] * 4, axis=1)
    sine = jnp.concatenate([sin_ref[...]] * 4, axis=1)
    turned = projected * cosine + swapped(projected) * sine
    q_out[...] = (turned * HEAD_DIM ** (-0.5)).astype(BF)
    tile = turned[:, 384:512]
    lane = lax.broadcasted_iota(jnp.int32, (SHARE, 128), 1)
    low = lane < 64
    own_kv[0] = jnp.where(low, pltpu.roll(tile, 64, 1), tile).astype(BF)
    double = (
        lax.rem(lax.broadcasted_iota(jnp.int32, (64, 128), 1), 64)
        == lax.broadcasted_iota(jnp.int32, (64, 128), 0)
    ).astype(F32).astype(BF)
    own_kv[1] = dot(values, double).astype(BF)
    kv_copies = [
        go(
            own_kv,
            kv_out.at[:, (4 - i) * SHARE : (5 - i) * SHARE, :],
            sem_kv.at[0, i - 1],
            sem_kv.at[1, i - 1],
            **near(i),
        )
        for i in (1, 2, 3, 4)
    ]
    kv_out[:, MAXLEN : MAXLEN + SHARE, :] = own_kv[...]
    for w in (2, 3, 4):
        pass_on(w, fetched[w])
    for copy in kv_copies:
        copy.wait_recv()
    cot_copies = [
        go(cot_ref, cot_all.at[r], sem_cot.at[0, k - 1], sem_cot.at[1, k - 1], row=q)
        for k, q in (peers[0], peers[2], peers[1])
    ]
    for m in range(HEADS // GROUPS):
        at = 128 * (m // 2)
        mine = low if m % 2 == 0 else jnp.logical_not(low)
        query = jnp.where(mine, q_out[:, at : at + 128].astype(F32), 0.0).astype(BF)
        scores = dot_nt(query, kv_out[0]) + mask[...]
        peak = jnp.max(scores, axis=1, keepdims=True)
        powered = jnp.exp(scores - peak)
        total = jnp.sum(powered, axis=1, keepdims=True)
        probs = (powered * (1.0 / total)).astype(BF)
        lse_out[m] = peak + jnp.log(total)
        mixed = dot(probs, kv_out[1])
        if m == 6:
            att_out[:, 384:448] = mixed[:, 0:64].astype(BF)
        elif m % 2 == 0:
            even = mixed
        else:
            att_out[:, at : at + 128] = jnp.where(low, even, mixed).astype(BF)
    shared[1] = share(1, fetched[1])
    shared[1].wait_recv()
    for j in range(4):
        c_send[j] = dot(att_out[...], outw_full[j]).astype(BF)
    cross = rcopy(c_send, c_in, sem_c.at[0], sem_c.at[1], col=1 - c)
    cross.start()
    for w in (2, 3, 4):
        shared[w] = share(w, fetched[w])
    cross.wait_recv()
    square = jnp.zeros((SHARE, 1), F32)
    for j in range(4):
        value = x_out[j].astype(F32) + (
            c_send[j].astype(F32) + c_in[j].astype(F32)
        )
        mid_out[j] = value
        square += jnp.sum(value * value, axis=1, keepdims=True)
    rate = lax.rsqrt(square / D + EPS)
    for j in range(4):
        ns_all[j, span(r), :] = (mid_out[j] * rate * gains_full[j, 1:2, :]).astype(BF)

    right, across, left = [q for _, q in peers]

    def spread(blocks, source, index, q):
        part = ns_all.at[blocks, span(source), :]
        return go(part, part, sem_ag.at[0, index], sem_ag.at[1, index], row=q)

    every, front_half, back_half = pl.ds(0, 4), pl.ds(0, 2), pl.ds(2, 2)
    from_left = spread(every, r, 0, right)
    from_right = spread(every, r, 1, left)
    for copy in cot_copies:
        copy.wait_recv()
    for w in (2, 3, 4):
        shared[w].wait_recv()
        shared[w].wait_send()
        finish(w, fetched[w])
    live = jnp.where(r < 3, 1.0, 0.0)
    extra = 4 * WIN - HALF_FF
    for j in range(4):
        gate_full[j, :, 0:extra] = (gate_full[j, :, 0:extra].astype(F32) * live).astype(BF)
        up_full[j, :, 0:extra] = (up_full[j, :, 0:extra].astype(F32) * live).astype(BF)
        cot_out[j] = cot_all[j, span(r), :]

    def feed(k, q, arrived):
        grad_hidden = dot_nt(cot_all[0, span(q), :], down_full[0])
        for j in range(1, 4):
            grad_hidden += dot_nt(cot_all[j, span(q), :], down_full[j])
        arrived()
        gate = dot(ns_all[0, span(q), :], gate_full[0])
        up = dot(ns_all[0, span(q), :], up_full[0])
        for j in range(1, 4):
            gate += dot(ns_all[j, span(q), :], gate_full[j])
            up += dot(ns_all[j, span(q), :], up_full[j])
        sigma = 1.0 / (1.0 + jnp.exp(-gate))
        silu = gate * sigma
        hid[span(q), :] = (silu * up).astype(BF)
        g_gate = (grad_hidden * up * (sigma + silu * (1.0 - sigma))).astype(BF)
        g_up = (grad_hidden * silu).astype(BF)
        gg[span(q), :] = g_gate
        gu[span(q), :] = g_up
        for j in range(4):
            sp_send[k, j] = (
                dot_nt(g_gate, gate_full[j]) + dot_nt(g_up, up_full[j])
            ).astype(BF)
        if k:
            return go(
                sp_send.at[k],
                sp_in.at[k - 1],
                sem_sp.at[0, k - 1],
                sem_sp.at[1, k - 1],
                row=q,
            )

    forwarded = []

    def neighbours_here():
        from_left.wait_recv()
        forwarded.append(spread(front_half, left, 2, right))
        from_right.wait_recv()
        forwarded.append(spread(back_half, right, 3, left))

    def opposite_here():
        for copy in forwarded:
            copy.wait_recv()

    feed(0, r, lambda: None)
    back = {}
    back[1] = feed(1, right, neighbours_here)
    back[3] = feed(3, left, lambda: None)
    back[2] = feed(2, across, opposite_here)

    grads_out[:, :, FEAT:PADF, :] = jnp.zeros((3, 4, PADF - FEAT, WIN), BF)
    for j in range(4):
        grads_out[0, j, 0:FEAT, :] = dot_tn(ns_all[j], gg[...]).astype(BF)
        grads_out[1, j, 0:FEAT, :] = dot_tn(ns_all[j], gu[...]).astype(BF)
    total = sp_send[0].astype(F32)
    for k in (1, 3, 2):
        back[k].wait_recv()
        total += sp_in[k - 1].astype(F32)
    cross.wait_send()
    c_send[...] = total.astype(BF)
    cross_two = go(c_send, second_in, sem_cs.at[0], sem_cs.at[1], col=1 - c)
    for j in range(4):
        grads_out[2, j, 0:FEAT, :] = dot_tn(cot_all[j], hid[...]).astype(BF)
        for q in range(4):
            op_out[j, q * SHARE : (q + 1) * SHARE, :] = dot(
                hid[q * SHARE : (q + 1) * SHARE, :], down_full[j]
            ).astype(BF)
        op_out[j, span(r), :] = (
            op_out[j, span(r), :].astype(F32) + 0.5 * mid_out[j]
        ).astype(BF)
    cross_two.wait_recv()
    second_out[...] = c_send[...].astype(F32) + second_in[...].astype(F32)
    for copy in pending:
        copy.wait_send()


def forward(*operands):
    dma = pltpu.SemaphoreType.DMA
    shape = jax.ShapeDtypeStruct
    width = MAXLEN + SHARE
    blocked = pltpu.VMEM((4, SHARE, FEAT), BF)
    return vmem_call(
        forward_kernel,
        12,
        (
            shape((4, SHARE, FEAT), BF),
            shape((4, SHARE, FEAT), BF),
            shape((SHARE, 512), BF),
            shape((2, width, 128), BF),
            shape((HEADS // GROUPS, SHARE, 1), F32),
            shape((SHARE, 448), BF),
            shape((4, SHARE, FEAT), F32),
            shape((4, FEAT, 576), BF),
            shape((4, 448, FEAT), BF),
            shape((4, 8, FEAT), F32),
            shape((4, SHARE, FEAT), BF),
            shape((4, SHARE, FEAT), F32),
            shape((4, SHARD, FEAT), BF),
            shape((3, 4, PADF, WIN), BF),
        ),
        [
            pltpu.VMEM((4, FEAT, WIN), BF),
            pltpu.VMEM((4, FEAT, WIN), BF),
            pltpu.VMEM((4, WIN, FEAT), BF),
            pltpu.VMEM((4, SHARD, FEAT), BF),
            pltpu.VMEM((SHARE, width), F32),
            pltpu.VMEM((2, SHARE, 128), BF),
            blocked,
            blocked,
            blocked,
            pltpu.VMEM((4, SHARD, FEAT), BF),
            pltpu.VMEM((SHARD, WIN), BF),
            pltpu.VMEM((SHARD, WIN), BF),
            pltpu.VMEM((SHARD, WIN), BF),
            pltpu.VMEM((4, 4, SHARE, FEAT), BF),
            pltpu.VMEM((3, 4, SHARE, FEAT), BF),
            dma((2, 3)),
            dma((2, 3)),
            dma((2, 5, 3)),
            dma((2, 3, 3, 3)),
            dma((2, 5)),
            dma((2, 3)),
            dma((2, 4)),
            dma((2,)),
            dma((2, 4)),
            dma((2, 3)),
            dma((2,)),
            dma((5,)),
        ],
        0,
    )(*operands)


class GradSum:
    def __init__(self, t, source, out, joined, wide_first, place, buffers, sems, go):
        self.t, self.source, self.out, self.joined, self.go = t, source, out, joined, go
        self.r, d = place
        self.core = lax.rem(d, 2)
        y = lax.rem(d // 2, 2)
        x = d // 4
        self.sibling = d + 1 - 2 * self.core
        along_x = [
            (k, lax.rem(x + k, 4), lax.rem(x + k, 4) * 4 + lax.rem(d, 4)) for k in (1, 2, 3)
        ]
        along_y = [(1, 1 - y, d + 2 - 4 * y)]
        if wide_first:
            self.first, self.second = (along_x, x, 32), (along_y, y, 16)
        else:
            self.first, self.second = (along_y, y, 64), (along_x, x, 16)
        self.at_first = self.core * 128 + self.first[1] * self.first[2]
        self.at = self.at_first + self.second[1] * 16
        self.core_in, self.part, self.low, self.in1, self.low2, self.in2, self.mine, self.z_in = [
            buffer.at[t] for buffer in buffers
        ]
        self.sem = lambda stage, k: (sems.at[0, t, stage, k - 1], sems.at[1, t, stage, k - 1])
        self.waiting = []
        self.done = 0

    def rows(self, start, size):
        return pl.ds(pl.multiple_of(start, 16), size)

    def settle(self):
        for copy in self.waiting:
            copy.wait_recv()
        self.waiting = []

    def send(self, source, target, stage, k, **device):
        self.waiting.append(self.go(source, target, *self.sem(stage, k), **device))

    def step(self):
        self.settle()
        getattr(self, "step%d" % self.done)()
        self.done += 1

    def step0(self):
        self.send(
            self.source.at[:, self.rows((1 - self.core) * 128, 128), :],
            self.core_in,
            0,
            1,
            dp=self.sibling,
        )

    def step1(self):
        peers, own, unit = self.first
        total = self.source[:, self.rows(self.core * 128, 128), :].astype(F32)
        total = total + self.core_in[...].astype(F32)
        self.part[...] = total
        self.low[...] = total.astype(BF)
        for k, index, device in peers:
            self.send(
                self.low.at[:, self.rows(index * unit, unit), :],
                self.in1.at[:, (k - 1) * unit : k * unit, :],
                1,
                k,
                dp=device,
            )

    def step2(self):
        peers, own, unit = self.first
        total = self.part[:, self.rows(own * unit, unit), :]
        for k, _, _ in peers:
            total = total + self.in1[:, (k - 1) * unit : k * unit, :].astype(F32)
        self.part[:, 0:unit, :] = total
        self.low2[:, 0:unit, :] = total.astype(BF)
        peers, own, unit = self.second
        for k, index, device in peers:
            self.send(
                self.low2.at[:, self.rows(index * unit, unit), :],
                self.in2.at[:, (k - 1) * unit : k * unit, :],
                2,
                k,
                dp=device,
            )

    def step3(self):
        peers, own, unit = self.second
        total = self.part[:, self.rows(own * unit, unit), :]
        for k, _, _ in peers:
            total = total + self.in2[:, (k - 1) * unit : k * unit, :].astype(F32)
        self.mine[...] = total.astype(BF)
        for k in (1, 2, 3):
            q = lax.rem(self.r + k, 4)
            self.send(self.mine.at[q], self.z_in.at[self.r], 3, k, row=q)
        self.z_in[self.r] = self.mine[self.r]

    def step4(self):
        here = self.rows(self.at, 16)
        if self.joined:
            for q in range(3):
                self.out[here, q * WIN : (q + 1) * WIN] = self.z_in[q]
            self.out[here, 3 * WIN : HALF_FF] = self.z_in[3][:, 4 * WIN - HALF_FF :]
        else:
            total = self.z_in[0].astype(F32)
            for q in range(1, 4):
                total = total + self.z_in[q].astype(F32)
            self.out[here, :] = total.astype(BF)
        self.spread(self.second[0], self.at, 16, 4)

    def spread(self, peers, start, size, stage):
        block = self.out.at[self.rows(start, size), :]
        for k, _, device in peers:
            self.send(block, block, stage, k, dp=device)

    def step5(self):
        self.spread(self.first[0], self.at_first, self.first[2], 5)

    def step6(self):
        self.spread([(1, 0, self.sibling)], self.core * 128, 128, 6)

    def step7(self):
        pass


def back_kernel(
    second_ref,
    mid_ref,
    cot_ref,
    x_ref,
    nf_ref,
    q_ref,
    kv_ref,
    lse_ref,
    att_ref,
    proj_full,
    outw_full,
    gains_full,
    cos_ref,
    sin_ref,
    start_ref,
    ff_ref,
    op_ref,
    block_out,
    input_out,
    ff_out,
    outw_out,
    proj_out,
    small_out,
    mask,
    g_mid,
    g_branch,
    g_att,
    dq,
    dk,
    dv,
    dkv,
    dkv_in,
    gp,
    gv,
    c_send,
    c_in,
    op_in,
    co_send,
    co_in,
    own_input,
    outw_grad,
    proj_grad,
    small,
    small_in,
    small_x,
    small_z,
    core_in,
    part,
    low_buf,
    in1,
    low2,
    in2,
    mine,
    z_in,
    sem_flow,
    sem_kv,
    sem_c,
    sem_in,
    sem_s,
    sem_op,
    sem_co,
):
    d = lax.axis_index("dp")
    r = lax.axis_index("row")
    c = lax.axis_index("col")
    core = lax.rem(d, 2)
    y = lax.rem(d // 2, 2)
    x = d // 4
    sibling = d + 1 - 2 * core
    other_y = d + 2 - 4 * y
    x_peers = [(k, lax.rem(x + k, 4) * 4 + lax.rem(d, 4)) for k in (1, 2, 3)]
    row_peers = [(k, lax.rem(r + k, 4)) for k in (1, 2, 3)]
    block = 4 * d + r
    near = lambda i: {
        "dp": lax.rem((block + 64 + i) // 4, 16),
        "row": lax.rem(r + 4 + i, 4),
    }
    greet(
        [{"row": q} for _, q in row_peers]
        + [{"dp": p} for _, p in x_peers]
        + [{"col": 1 - c}, {"dp": sibling}, {"dp": other_y}]
        + [near(i) for i in (1, 2, 3, 4, -1, -2, -3, -4)]
    )
    pending = []

    def go(*args, **device):
        copy = rcopy(*args, **device)
        copy.start()
        pending.append(copy)
        return copy

    span = lambda q: pl.ds(pl.multiple_of(q * SHARE, SHARE), SHARE)
    buffers = (core_in, part, low_buf, in1, low2, in2, mine, z_in)
    flows = [
        GradSum(t, source, out, joined, wide_first, (r, d), buffers, sem_flow, go)
        for t, source, out, joined, wide_first in (
            (0, ff_ref.at[0], ff_out.at[0], True, True),
            (1, ff_ref.at[1], ff_out.at[1], True, False),
            (2, ff_ref.at[2], ff_out.at[2], True, True),
            (3, outw_grad, outw_out, False, False),
            (4, proj_grad, proj_out, False, True),
        )
    ]
    early, tail = flows[:4], flows[4]
    for flow in early[:3]:
        flow.step()

    def scatter(k, q):
        return go(
            op_ref.at[q], op_in.at[k - 1], sem_op.at[0, k - 1], sem_op.at[1, k - 1], row=q
        )

    op_copies = [scatter(*row_peers[0]), scatter(*row_peers[2])]

    small[...] = jnp.zeros_like(small)
    square = jnp.zeros((SHARE, 1), F32)
    inner = jnp.zeros((SHARE, 1), F32)
    for j in range(4):
        value = mid_ref[j]
        square += jnp.sum(value * value, axis=1, keepdims=True)
        inner += jnp.sum(second_ref[j] * gains_full[j, 1:2, :] * value, axis=1, keepdims=True)
    rate = lax.rsqrt(square / D + EPS)
    scale = rate * rate * rate * inner / D
    for j in range(4):
        value = mid_ref[j]
        grad = second_ref[j]
        small[j, 1:2, 0:FEAT] = jnp.sum(grad * value * rate, axis=0, keepdims=True)
        total = (
            cot_ref[j].astype(F32)
            + rate * (grad * gains_full[j, 1:2, :])
            - value * scale
        )
        g_mid[j] = total
        g_branch[j] = total.astype(BF)
    grad_att = dot_nt(g_branch[0], outw_full[0])
    for j in range(1, 4):
        grad_att += dot_nt(g_branch[j], outw_full[j])
    g_att[:, 448:512] = jnp.zeros((SHARE, 64), BF)
    g_att[:, 0:448] = grad_att.astype(BF)
    for flow in early[:3]:
        flow.step()
    outw_grad[...] = jnp.zeros_like(outw_grad)
    for j in range(4):
        outw_grad[j, 0:FEAT, 0:448] = dot_tn(g_branch[j], att_ref[...]).astype(BF)
    early[3].step()
    query_at = lax.broadcasted_iota(jnp.int32, (SHARE, 1), 0) + MAXLEN
    key_at = lax.broadcasted_iota(jnp.int32, (SHARE, MAXLEN + SHARE), 1)
    mask[...] = jnp.where(
        (key_at >= start_ref[...]) & (key_at <= query_at), 0.0, -1e30
    )

    lane = lax.broadcasted_iota(jnp.int32, (SHARE, 128), 1)
    low = lane < 64
    for m in range(HEADS // GROUPS):
        at = 128 * (m // 2)
        mine_lanes = low if m % 2 == 0 else jnp.logical_not(low)
        pick = lambda ref: jnp.where(
            mine_lanes, ref[:, at : at + 128].astype(F32), 0.0
        ).astype(BF)
        query, grad = pick(q_ref), pick(g_att)
        probs = jnp.exp(dot_nt(query, kv_ref[0]) + mask[...] - lse_ref[m])
        grad_probs = dot_nt(grad, kv_ref[1])
        inner = jnp.sum(probs * grad_probs, axis=1, keepdims=True)
        grad_scores = (probs * (grad_probs - inner)).astype(BF)
        grad_v = dot_tn(probs.astype(BF), grad)
        grad_k = dot_tn(grad_scores, query)
        if m == 0:
            dv[...] = grad_v
            dk[...] = grad_k
        else:
            dv[...] += grad_v
            dk[...] += grad_k
        grad_q = dot(grad_scores, kv_ref[0]) * HEAD_DIM ** (-0.5)
        if m % 2 == 0:
            dq[:, at : at + 128] = grad_q
        else:
            dq[:, at : at + 128] = jnp.where(low, dq[:, at : at + 128], grad_q)
        if m == 1:
            early[3].step()
    wide_low = lax.broadcasted_iota(jnp.int32, (MAXLEN + SHARE, 128), 1) < 64
    dkv[...] = jnp.where(
        wide_low,
        dk[...] + pltpu.roll(dk[...], 64, 1),
        dv[...] + pltpu.roll(dv[...], 64, 1),
    ).astype(BF)
    kv_copies = [
        go(
            dkv.at[(4 - i) * SHARE : (5 - i) * SHARE, :],
            dkv_in.at[i - 1],
            sem_kv.at[0, i - 1],
            sem_kv.at[1, i - 1],
            **near(-i),
        )
        for i in (1, 2, 3, 4)
    ]
    for flow in early:
        flow.step()
    total = dkv[MAXLEN : MAXLEN + SHARE, :].astype(F32)
    for i in (1, 2, 3, 4):
        kv_copies[i - 1].wait_recv()
        total += dkv_in[i - 1].astype(F32)
    op_copies.append(scatter(*row_peers[1]))
    turned = pltpu.roll(total, 64, 1)
    dq[:, 384:512] = jnp.where(low, dq[:, 384:512], turned)
    gv[...] = turned[:, 0:64].astype(BF)
    cosine = jnp.concatenate([cos_ref[...]] * 4, axis=1)
    sine = jnp.concatenate([sin_ref[...]] * 4, axis=1)
    gp[...] = (dq[...] * cosine - swapped(dq[...]) * sine).astype(BF)
    for j in range(4):
        c_send[j] = (
            dot_nt(gp[...], proj_full[j, :, 0:512])
            + dot_nt(gv[...], proj_full[j, :, 512:576])
        ).astype(BF)
    cross = go(c_send, c_in, sem_c.at[0], sem_c.at[1], col=1 - c)
    proj_grad[...] = jnp.zeros_like(proj_grad)
    for j in range(4):
        proj_grad[j, 0:FEAT, 0:512] = dot_tn(nf_ref[j], gp[...]).astype(BF)
        proj_grad[j, 0:FEAT, 512:576] = dot_tn(nf_ref[j], gv[...]).astype(BF)
    tail.step()
    bias_a = jnp.sum(gp[...].astype(F32), axis=0, keepdims=True)
    bias_b = jnp.sum(gv[...].astype(F32), axis=0, keepdims=True)
    for j in range(4):
        small[j, 2:3, 0:512] = bias_a
        small[j, 2:3, 512:576] = bias_b
    for flow in early:
        flow.step()
    tail.step()

    square = jnp.zeros((SHARE, 1), F32)
    for j in range(4):
        value = x_ref[j].astype(F32)
        square += jnp.sum(value * value, axis=1, keepdims=True)
    rate = lax.rsqrt(square / D + EPS)
    cross.wait_recv()
    inner = jnp.zeros((SHARE, 1), F32)
    for j in range(4):
        grad = c_send[j].astype(F32) + c_in[j].astype(F32)
        inner += jnp.sum(
            grad * gains_full[j, 0:1, :] * x_ref[j].astype(F32), axis=1, keepdims=True
        )
    scale = rate * rate * rate * inner / D
    for j in range(4):
        value = x_ref[j].astype(F32)
        grad = c_send[j].astype(F32) + c_in[j].astype(F32)
        small[j, 0:1, 0:FEAT] = jnp.sum(grad * value * rate, axis=0, keepdims=True)
        own_input[j] = (
            g_mid[j] + rate * (grad * gains_full[j, 0:1, :]) - value * scale
        ).astype(BF)
    in_copies = [
        go(
            own_input.at[q],
            input_out.at[r],
            sem_in.at[0, k - 1],
            sem_in.at[1, k - 1],
            row=q,
        )
        for k, q in row_peers
    ]
    input_out[r] = own_input[r]

    total = op_ref[r].astype(F32)
    for copy in op_copies:
        copy.wait_recv()
    for k in range(3):
        total += op_in[k].astype(F32)
    co_send[...] = total.astype(BF)
    final = go(co_send, co_in, sem_co.at[0], sem_co.at[1], col=1 - c)

    def swap(stage, source, target, k, **device):
        return go(source, target, sem_s.at[0, stage, k - 1], sem_s.at[1, stage, k - 1], **device)

    copy = swap(0, small, small_in.at[0], 1, dp=sibling)
    for flow in early:
        flow.step()
    tail.step()
    copy.wait_recv()
    small_x[0] = small[...] + small_in[0]
    copies = [swap(1, small_x.at[0], small_in.at[k], k, dp=p) for k, p in x_peers]
    for flow in early:
        flow.step()
    tail.step()
    for copy in copies:
        copy.wait_recv()
    small_x[1] = small_x[0] + small_in[1] + small_in[2] + small_in[3]
    copy = swap(2, small_x.at[1], small_in.at[4], 1, dp=other_y)
    tail.step()
    copy.wait_recv()
    small_x[2] = small_x[1] + small_in[4]
    copies = [swap(3, small_x.at[2, q], small_z.at[r], k, row=q) for k, q in row_peers]
    small_z[r] = small_x[2, r]
    tail.step()
    for flow in early:
        flow.step()
    for copy in copies:
        copy.wait_recv()
    small_out[...] = small_z[0] + small_z[1] + small_z[2] + small_z[3]
    tail.step()
    for flow in early:
        flow.step()
    tail.step()
    for copy in in_copies:
        copy.wait_recv()
    final.wait_recv()
    block_out[...] = (co_send[...].astype(F32) + co_in[...].astype(F32)).astype(BF)
    for copy in pending:
        copy.wait_send()


def back(*operands):
    dma = pltpu.SemaphoreType.DMA
    shape = jax.ShapeDtypeStruct
    width = MAXLEN + SHARE
    blocked = pltpu.VMEM((4, SHARE, FEAT), BF)
    count = 5
    return vmem_call(
        back_kernel,
        17,
        (
            shape((SHARD, FEAT), BF),
            shape((4, SHARE, FEAT), BF),
            shape((3, PADF, HALF_FF), BF),
            shape((PADF, WIN), BF),
            shape((PADF, WIN), BF),
            shape((8, WIN), F32),
        ),
        [
            pltpu.VMEM((SHARE, width), F32),
            pltpu.VMEM((4, SHARE, FEAT), F32),
            blocked,
            pltpu.VMEM((SHARE, 512), BF),
            pltpu.VMEM((SHARE, 512), F32),
            pltpu.VMEM((width, 128), F32),
            pltpu.VMEM((width, 128), F32),
            pltpu.VMEM((width, 128), BF),
            pltpu.VMEM((4, SHARE, 128), BF),
            pltpu.VMEM((SHARE, 512), BF),
            pltpu.VMEM((SHARE, 64), BF),
            blocked,
            blocked,
            pltpu.VMEM((3, SHARD, FEAT), BF),
            pltpu.VMEM((SHARD, FEAT), BF),
            pltpu.VMEM((SHARD, FEAT), BF),
            blocked,
            pltpu.VMEM((4, PADF, WIN), BF),
            pltpu.VMEM((4, PADF, WIN), BF),
            pltpu.VMEM((4, 8, WIN), F32),
            pltpu.VMEM((5, 4, 8, WIN), F32),
            pltpu.VMEM((3, 4, 8, WIN), F32),
            pltpu.VMEM((4, 8, WIN), F32),
            pltpu.VMEM((count, 4, 128, WIN), BF),
            pltpu.VMEM((count, 4, 128, WIN), F32),
            pltpu.VMEM((count, 4, 128, WIN), BF),
            pltpu.VMEM((count, 4, 96, WIN), BF),
            pltpu.VMEM((count, 4, 64, WIN), BF),
            pltpu.VMEM((count, 4, 48, WIN), BF),
            pltpu.VMEM((count, 4, 16, WIN), BF),
            pltpu.VMEM((count, 4, 16, WIN), BF),
            dma((2, count, 7, 3)),
            dma((2, 4)),
            dma((2,)),
            dma((2, 3)),
            dma((2, 4, 3)),
            dma((2, 3)),
            dma((2,)),
        ],
        1,
    )(*operands)


def body(
    activations,
    starts,
    first_gain,
    project_weight,
    project_bias,
    output_weight,
    second_gain,
    gate_weight,
    up_weight,
    down_weight,
    cotangent,
):
    r = lax.axis_index("row")
    shard = lax.axis_index("dp")
    query_width = HEADS // GROUPS * HEAD_DIM

    base = shard * SHARD + r * SHARE
    start_window = (
        lax.dynamic_slice_in_dim(starts, r * SHARE, SHARE, 0) - base + MAXLEN
    )[:, None]
    positions = (MAXLEN + jnp.arange(SHARE, dtype=jnp.int32))[:, None] - start_window
    half = HEAD_DIM // 2
    freqs = 1000000.0 ** (-jnp.arange(half, dtype=F32) * 2.0 / HEAD_DIM)
    angle = positions.astype(F32) * jnp.tile(freqs, 4)[None, :]
    cosine = jnp.cos(angle)
    sine = jnp.sin(angle) * jnp.tile(jnp.repeat(jnp.array([-1.0, 1.0], F32), half), 2)[None, :]
    gains = jnp.pad(jnp.stack([first_gain, second_gain]), ((0, 6), (0, 0)))
    (
        x_low,
        normed_first,
        queries,
        kv,
        lse,
        attended,
        middle,
        project_full,
        output_full,
        gains_full,
        cot_own,
        grad_second,
        out_partial,
        ff_grads,
    ) = forward(
        activations,
        cotangent,
        project_weight,
        output_weight,
        gate_weight,
        up_weight,
        down_weight,
        gains,
        project_bias[None, :],
        cosine,
        sine,
        start_window,
    )
    block_output, input_grad, ff_sum, outw_sum, project_sum, small = back(
        grad_second,
        middle,
        cot_own,
        x_low,
        normed_first,
        queries,
        kv,
        lse,
        attended,
        project_full,
        output_full,
        gains_full,
        cosine,
        sine,
        start_window,
        ff_grads,
        out_partial,
    )
    width = project_weight.shape[1]
    ff_sum = ff_sum[:, :FEAT].astype(F32)
    return (
        block_output,
        input_grad.reshape(SHARD, FEAT).astype(F32),
        small[0, :FEAT],
        project_sum[:FEAT, :width].astype(F32),
        small[2, :width],
        outw_sum[:FEAT, :query_width].astype(F32).T,
        small[1, :FEAT],
        ff_sum[0],
        ff_sum[1],
        ff_sum[2].T,
    )


def solution(mesh):
    return jax.shard_map(
        body,
        mesh=mesh,
        in_specs=(
            P("dp", "row"),
            P("dp"),
            P("row"),
            P("row", "col"),
            P("col"),
            P("col", "row"),
            P("row"),
            P("row", "col"),
            P("row", "col"),
            P("col", "row"),
            P("dp", "row"),
        ),
        out_specs=(
            P("dp", "row"),
            P("dp", "row"),
            P("row"),
            P("row", "col"),
            P("col"),
            P("col", "row"),
            P("row"),
            P("row", "col"),
            P("row", "col"),
            P("col", "row"),
        ),
        check_vma=False,
    )
```

profile of v0, /device:TPU:1, one launch (start us, length us, event | category | flops | bytes accessed | tf_op | source)
XLA Modules:
  0.0 243.3 jit_solution(7528612100222175625)
XLA Ops:
  0.6 0.0 copy-start
  0.7 0.8 broadcast_in_dim.11
  1.5 0.1 tile.14
  1.6 0.1 mul.41
  1.7 0.8 subtract_convert_fusion
  2.4 0.1 mul.38
  2.5 1.3 broadcast_in_dim.10.bias_ref
  3.8 1.3 select_maximum_fusion.gains_ref
  5.1 0.8 copy.31.start_ref
  5.9 1.2 fusion
  7.1 2.0 copy.28.act_ref
  9.1 2.0 copy.29.cot_ref
  11.2 0.0 copy-done
  11.2 1.5 copy.30.down_ref
  12.7 128.1 %shard_map.195 = (bf16[4,256,224]{2,1,0:T(8,128)(2,1)}, bf16[4,256,224]{2,1,0:T(8,128)(2,1)}, bf16[256,512]{1,0:T(8,128)(2,1)}, bf16[2,1280,128]{2,1,0:T(8,128)(...) custom-call(bf16[1024,224]{1,0:T(8,128)(2,1)} %copy.28.act_ref, ...), custom_call_target="tpu_custom_call" | custom-call | tf_op jit(solution)/shard_map/pallas_call | solution.py:480
  140.8 88.1 %shard_map.196 = (bf16[1024,224]{1,0:T(8,128)(2,1)}, bf16[4,256,224]{2,1,0:T(8,128)(2,1)}, bf16[3,256,2432]{2,1,0:T(8,128)(2,1)}, bf16[256,640]{1,0:T(8,128)(2,1...) custom-call(f32[4,256,224]{2,1,0:T(8,128)} %get-tuple-element.30.second_ref, f32[4,256,224]{2,1,0:T(8,128)} %get-tuple-element.31.mid_ref, ...), custom_call_target="tpu_custom_call" | custom-call | tf_op jit(solution)/shard_map/pallas_call | solution.py:968
  228.9 0.0 copy-start.2
  228.9 0.0 copy-start.1
  228.9 2.1 copy.33
  231.0 1.3 fusion.1
  232.3 1.3 slice_reduce_fusion
  233.7 1.0 convert_bitcast_fusion
  234.6 1.0 copy.35
  235.6 0.0 copy-done.2
  235.6 0.8 slice_convert_fusion.1
  236.4 0.0 copy-done.1
  236.4 0.1 bitcast_convert_fusion
  236.6 1.3 copy.34
  237.8 2.4 slice_convert_fusion
  240.2 2.9 %slice_bitcast_fusion = (f32[2432,224]{0,1:T(8,128)}, f32[224,2432]{1,0:T(8,128)}, f32[224,2432]{1,0:T(8,128)}) fusion(f32[3,224,2432]{2,1,0:T(8,128)S(1)} %slice_convert_fusion), kind=kLoop, calls=%fused_computation.1 | loop fusion | bytes 13074432 | tf_op jit(solution)/shard_map/transpose | solution.py:1111
  (3 shorter events, 0.0 us)
Async XLA Ops:
  0.6 10.5 %copy-start = (bf16[2432,224]{0,1:T(8,128)(2,1)S(1)}, bf16[2432,224]{0,1:T(8,128)(2,1)}, u32[]{:S(2)}) copy-start(bf16[2432,224]{0,1:T(8,128)(2,1)} %param.21) | copy-start | bytes 3268612
  228.9 6.7 %copy-start.2 = (bf16[256,640]{1,0:T(8,128)(2,1)S(1)}, bf16[256,640]{1,0:T(8,128)(2,1)}, u32[]{:S(2)}) copy-start(bf16[256,640]{1,0:T(8,128)(2,1)} %get-tuple-element.47) | copy-start | bytes 983044
  228.9 7.6 %copy-start.1 = (bf16[4,256,224]{2,1,0:T(8,128)(2,1)S(1)}, bf16[4,256,224]{2,1,0:T(8,128)(2,1)}, u32[]{:S(2)}) copy-start(bf16[4,256,224]{2,1,0:T(8,128)(2,1)} %get-tuple-element.45) | copy-start | bytes 1376260
where the time goes:
time: 247 us; the launch traced here: 243 us
  Pallas kernels  216 us (87%)
  local copies, waits for them, and re-layouts  18.6 us (8%)
  other arithmetic  7.65 us (3%)
    pallas_call x1, Pallas kernels, forward(): vmem_call(forward_kernel, 12, (shape((4, SHARE, FEAT), BF), shape((4, SHA...  128 us
    pallas_call x1, Pallas kernels, back(): vmem_call(back_kernel, 17, (shape((SHARD, FEAT), BF), shape((4, SHARE, FE...  88.1 us
    unnamed x12, local copies, waits for them, and re-layouts  9.85 us

commit v1 on v0

--- a/solution.py
+++ b/solution.py
@@ -72,6 +72,134 @@
         ),
         cost_estimate=cost,
     )
+
+
+class GradSum:
+    def __init__(self, t, source, out, joined, wide_first, place, buffers, sems, go):
+        self.t, self.source, self.out, self.joined, self.go = t, source, out, joined, go
+        self.r, d = place
+        self.core = lax.rem(d, 2)
+        y = lax.rem(d // 2, 2)
+        x = d // 4
+        self.sibling = d + 1 - 2 * self.core
+        along_x = [
+            (k, lax.rem(x + k, 4), lax.rem(x + k, 4) * 4 + lax.rem(d, 4)) for k in (1, 2, 3)
+        ]
+        along_y = [(1, 1 - y, d + 2 - 4 * y)]
+        if wide_first:
+            self.first, self.second = (along_x, x, 32), (along_y, y, 16)
+        else:
+            self.first, self.second = (along_y, y, 64), (along_x, x, 16)
+        self.at_first = self.core * 128 + self.first[1] * self.first[2]
+        self.at = self.at_first + self.second[1] * 16
+        self.core_in, self.part, self.low, self.in1, self.low2, self.in2, self.mine, self.z_in = [
+            buffer.at[t] if buffer is not None else None for buffer in buffers
+        ]
+        self.sem = lambda stage, k: (sems.at[0, t, stage, k - 1], sems.at[1, t, stage, k - 1])
+        self.waiting = []
+        self.done = 0
+
+    def rows(self, start, size):
+        return pl.ds(pl.multiple_of(start, 16), size)
+
+    def settle(self):
+        for copy in self.waiting:
+            copy.wait_recv()
+        self.waiting = []
+
+    def send(self, source, target, stage, k, **device):
+        self.waiting.append(self.go(source, target, *self.sem(stage, k), **device))
+
+    def step(self):
+        self.settle()
+        getattr(self, "step%d" % self.done)()
+        self.done += 1
+
+    def step0(self):
+        self.send(
+            self.source.at[:, self.rows((1 - self.core) * 128, 128), :],
+            self.core_in,
+            0,
+            1,
+            dp=self.sibling,
+        )
+
+    def step1(self):
+        peers, own, unit = self.first
+        total = self.source[:, self.rows(self.core * 128, 128), :].astype(F32)
+        total = total + self.core_in[...].astype(F32)
+        self.part[...] = total
+        self.low[...] = total.astype(BF)
+        for k, index, device in peers:
+            self.send(
+                self.low.at[:, self.rows(index * unit, unit), :],
+                self.in1.at[:, (k - 1) * unit : k * unit, :],
+                1,
+                k,
+                dp=device,
+            )
+
+    def step2(self):
+        peers, own, unit = self.first
+        total = self.part[:, self.rows(own * unit, unit), :]
+        for k, _, _ in peers:
+            total = total + self.in1[:, (k - 1) * unit : k * unit, :].astype(F32)
+        self.part[:, 0:unit, :] = total
+        self.low2[:, 0:unit, :] = total.astype(BF)
+        peers, own, unit = self.second
+        for k, index, device in peers:
+            self.send(
+                self.low2.at[:, self.rows(index * unit, unit), :],
+                self.in2.at[:, (k - 1) * unit : k * unit, :],
+                2,
+                k,
+                dp=device,
+            )
+
+    def step3(self):
+        self.reduce()
+        self.cross_rows()
+
+    def reduce(self):
+        self.settle()
+        peers, own, unit = self.second
+        total = self.part[:, self.rows(own * unit, unit), :]
+        for k, _, _ in peers:
+            total = total + self.in2[:, (k - 1) * unit : k * unit, :].astype(F32)
+        self.mine[...] = total.astype(BF)
+
+    def cross_rows(self):
+        for k in (1, 2, 3):
+            q = lax.rem(self.r + k, 4)
+            self.send(self.mine.at[q], self.z_in.at[self.r], 3, k, row=q)
+        self.z_in[self.r] = self.mine[self.r]
+
+    def step4(self):
+        here = self.rows(self.at, 16)
+        if self.joined:
+            for q in range(3):
+                self.out[here, q * WIN : (q + 1) * WIN] = self.z_in[q]
+            self.out[here, 3 * WIN : HALF_FF] = self.z_in[3][:, 4 * WIN - HALF_FF :]
+        else:
+            total = self.z_in[0].astype(F32)
+            for q in range(1, 4):
+                total = total + self.z_in[q].astype(F32)
+            self.out[here, :] = total.astype(BF)
+        self.spread(self.second[0], self.at, 16, 4)
+
+    def spread(self, peers, start, size, stage):
+        block = self.out.at[self.rows(start, size), :]
+        for k, _, device in peers:
+            self.send(block, block, stage, k, dp=device)
+
+    def step5(self):
+        self.spread(self.first[0], self.at_first, self.first[2], 5)
+
+    def step6(self):
+        self.spread([(1, 0, self.sibling)], self.core * 128, 128, 6)
+
+    def step7(self):
+        pass
 
 
 def swapped(values):
@@ -110,7 +238,7 @@
     cot_out,
     second_out,
     op_out,
-    grads_out,
+    mine_out,
     gate_full,
     up_full,
     down_full,
@@ -126,6 +254,13 @@
     gu,
     sp_send,
     sp_in,
+    grads,
+    core_in,
+    part,
+    low_buf,
+    in1,
+    low2,
+    in2,
     sem_x,
     sem_g,
     sem_w,
@@ -137,6 +272,7 @@
     sem_ag,
     sem_sp,
     sem_cs,
+    sem_flow,
     sem_l,
 ):
     d = lax.axis_index("dp")
@@ -145,6 +281,7 @@
     core = lax.rem(d, 2)
     x_at = d // 4
     sibling = d + 1 - 2 * core
+    other_y = d + 2 - 4 * lax.rem(d // 2, 2)
     x_peers = [(k, lax.rem(x_at + k, 4) * 4 + lax.rem(d, 4)) for k in (1, 2, 3)]
     block = 4 * d + r
     near = lambda i: {
@@ -154,7 +291,7 @@
     greet(
         [{"row": lax.rem(r + k, 4)} for k in (1, 2, 3)]
         + [{"dp": p} for _, p in x_peers]
-        + [{"col": 1 - c}, {"dp": sibling}]
+        + [{"col": 1 - c}, {"dp": sibling}, {"dp": other_y}]
         + [near(i) for i in (1, 2, 3, 4, -1, -2, -3, -4)]
     )
     pending = []
@@ -415,18 +552,22 @@
         g_up = (grad_hidden * silu).astype(BF)
         gg[span(q), :] = g_gate
         gu[span(q), :] = g_up
+        copies = []
         for j in range(4):
             sp_send[k, j] = (
                 dot_nt(g_gate, gate_full[j]) + dot_nt(g_up, up_full[j])
             ).astype(BF)
-        if k:
-            return go(
-                sp_send.at[k],
-                sp_in.at[k - 1],
-                sem_sp.at[0, k - 1],
-                sem_sp.at[1, k - 1],
-                row=q,
-            )
+            if k and j % 2:
+                copies.append(
+                    go(
+                        sp_send.at[k, j - 1 : j + 1],
+                        sp_in.at[k - 1, j - 1 : j + 1],
+                        sem_sp.at[0, k - 1, j // 2],
+                        sem_sp.at[1, k - 1, j // 2],
+                        row=q,
+                    )
+                )
+        return copies
 
     forwarded = []
 
@@ -446,19 +587,37 @@
     back[3] = feed(3, left, lambda: None)
     back[2] = feed(2, across, opposite_here)
 
-    grads_out[:, :, FEAT:PADF, :] = jnp.zeros((3, 4, PADF - FEAT, WIN), BF)
-    for j in range(4):
-        grads_out[0, j, 0:FEAT, :] = dot_tn(ns_all[j], gg[...]).astype(BF)
-        grads_out[1, j, 0:FEAT, :] = dot_tn(ns_all[j], gu[...]).astype(BF)
-    total = sp_send[0].astype(F32)
-    for k in (1, 3, 2):
-        back[k].wait_recv()
-        total += sp_in[k - 1].astype(F32)
+    buffers = (core_in, part, low_buf, in1, low2, in2, mine_out, None)
+    flows = [
+        GradSum(t, grads.at[t], None, True, True, (r, d), buffers, sem_flow, go)
+        for t in range(3)
+    ]
+    grads[:, :, FEAT:PADF, :] = jnp.zeros((3, 4, PADF - FEAT, WIN), BF)
+    for t, left_side, right_side in ((0, ns_all, gg), (1, ns_all, gu), (2, cot_all, hid)):
+        for j in range(4):
+            grads[t, j, 0:FEAT, :] = dot_tn(left_side[j], right_side[...]).astype(BF)
+        flows[t].step()
+        if t:
+            flows[t - 1].step()
+    flows[2].step()
     cross.wait_send()
-    c_send[...] = total.astype(BF)
-    cross_two = go(c_send, second_in, sem_cs.at[0], sem_cs.at[1], col=1 - c)
-    for j in range(4):
-        grads_out[2, j, 0:FEAT, :] = dot_tn(cot_all[j], hid[...]).astype(BF)
+    crosses = []
+    for h in (0, 2):
+        total = sp_send[0, h : h + 2].astype(F32)
+        for k in (1, 3, 2):
+            back[k][h // 2].wait_recv()
+            total += sp_in[k - 1, h : h + 2].astype(F32)
+        c_send[h : h + 2] = total.astype(BF)
+        crosses.append(
+            go(
+                c_send.at[h : h + 2],
+                second_in.at[h : h + 2],
+                sem_cs.at[0, h // 2],
+                sem_cs.at[1, h // 2],
+                col=1 - c,
+            )
+        )
+    for j in range(4):
         for q in range(4):
             op_out[j, q * SHARE : (q + 1) * SHARE, :] = dot(
                 hid[q * SHARE : (q + 1) * SHARE, :], down_full[j]
@@ -466,8 +625,13 @@
         op_out[j, span(r), :] = (
             op_out[j, span(r), :].astype(F32) + 0.5 * mid_out[j]
         ).astype(BF)
-    cross_two.wait_recv()
+    for flow in flows:
+        flow.step()
+    for copy in crosses:
+        copy.wait_recv()
     second_out[...] = c_send[...].astype(F32) + second_in[...].astype(F32)
+    for flow in flows:
+        flow.reduce()
     for copy in pending:
         copy.wait_send()
 
@@ -494,7 +658,7 @@
             shape((4, SHARE, FEAT), BF),
             shape((4, SHARE, FEAT), F32),
             shape((4, SHARD, FEAT), BF),
-            shape((3, 4, PADF, WIN), BF),
+            shape((3, 4, 16, WIN), BF),
         ),
         [
             pltpu.VMEM((4, FEAT, WIN), BF),
@@ -512,6 +676,13 @@
             pltpu.VMEM((SHARD, WIN), BF),
             pltpu.VMEM((4, 4, SHARE, FEAT), BF),
             pltpu.VMEM((3, 4, SHARE, FEAT), BF),
+            pltpu.VMEM((3, 4, PADF, WIN), BF),
+            pltpu.VMEM((3, 4, 128, WIN), BF),
+            pltpu.VMEM((3, 4, 128, WIN), F32),
+            pltpu.VMEM((3, 4, 128, WIN), BF),
+            pltpu.VMEM((3, 4, 96, WIN), BF),
+            pltpu.VMEM((3, 4, 64, WIN), BF),
+            pltpu.VMEM((3, 4, 48, WIN), BF),
             dma((2, 3)),
             dma((2, 3)),
             dma((2, 5, 3)),
@@ -521,133 +692,13 @@
             dma((2, 4)),
             dma((2,)),
             dma((2, 4)),
-            dma((2, 3)),
-            dma((2,)),
+            dma((2, 3, 2)),
+            dma((2, 2)),
+            dma((2, 3, 3, 3)),
             dma((5,)),
         ],
         0,
     )(*operands)
-
-
-class GradSum:
-    def __init__(self, t, source, out, joined, wide_first, place, buffers, sems, go):
-        self.t, self.source, self.out, self.joined, self.go = t, source, out, joined, go
-        self.r, d = place
-        self.core = lax.rem(d, 2)
-        y = lax.rem(d // 2, 2)
-        x = d // 4
-        self.sibling = d + 1 - 2 * self.core
-        along_x = [
-            (k, lax.rem(x + k, 4), lax.rem(x + k, 4) * 4 + lax.rem(d, 4)) for k in (1, 2, 3)
-        ]
-        along_y = [(1, 1 - y, d + 2 - 4 * y)]
-        if wide_first:
-            self.first, self.second = (along_x, x, 32), (along_y, y, 16)
-        else:
-            self.first, self.second = (along_y, y, 64), (along_x, x, 16)
-        self.at_first = self.core * 128 + self.first[1] * self.first[2]
-        self.at = self.at_first + self.second[1] * 16
-        self.core_in, self.part, self.low, self.in1, self.low2, self.in2, self.mine, self.z_in = [
-            buffer.at[t] for buffer in buffers
-        ]
-        self.sem = lambda stage, k: (sems.at[0, t, stage, k - 1], sems.at[1, t, stage, k - 1])
-        self.waiting = []
-        self.done = 0
-
-    def rows(self, start, size):
-        return pl.ds(pl.multiple_of(start, 16), size)
-
-    def settle(self):
-        for copy in self.waiting:
-            copy.wait_recv()
-        self.waiting = []
-
-    def send(self, source, target, stage, k, **device):
-        self.waiting.append(self.go(source, target, *self.sem(stage, k), **device))
-
-    def step(self):
-        self.settle()
-        getattr(self, "step%d" % self.done)()
-        self.done += 1
-
-    def step0(self):
-        self.send(
-            self.source.at[:, self.rows((1 - self.core) * 128, 128), :],
-            self.core_in,
-            0,
-            1,
-            dp=self.sibling,
-        )
-
-    def step1(self):
-        peers, own, unit = self.first
-        total = self.source[:, self.rows(self.core * 128, 128), :].astype(F32)
-        total = total + self.core_in[...].astype(F32)
-        self.part[...] = total
-        self.low[...] = total.astype(BF)
-        for k, index, device in peers:
-            self.send(
-                self.low.at[:, self.rows(index * unit, unit), :],
-                self.in1.at[:, (k - 1) * unit : k * unit, :],
-                1,
-                k,
-                dp=device,
-            )
-
-    def step2(self):
-        peers, own, unit = self.first
-        total = self.part[:, self.rows(own * unit, unit), :]
-        for k, _, _ in peers:
-            total = total + self.in1[:, (k - 1) * unit : k * unit, :].astype(F32)
-        self.part[:, 0:unit, :] = total
-        self.low2[:, 0:unit, :] = total.astype(BF)
-        peers, own, unit = self.second
-        for k, index, device in peers:
-            self.send(
-                self.low2.at[:, self.rows(index * unit, unit), :],
-                self.in2.at[:, (k - 1) * unit : k * unit, :],
-                2,
-                k,
-                dp=device,
-            )
-
-    def step3(self):
-        peers, own, unit = self.second
-        total = self.part[:, self.rows(own * unit, unit), :]
-        for k, _, _ in peers:
-            total = total + self.in2[:, (k - 1) * unit : k * unit, :].astype(F32)
-        self.mine[...] = total.astype(BF)
-        for k in (1, 2, 3):
-            q = lax.rem(self.r + k, 4)
-            self.send(self.mine.at[q], self.z_in.at[self.r], 3, k, row=q)
-        self.z_in[self.r] = self.mine[self.r]
-
-    def step4(self):
-        here = self.rows(self.at, 16)
-        if self.joined:
-            for q in range(3):
-                self.out[here, q * WIN : (q + 1) * WIN] = self.z_in[q]
-            self.out[here, 3 * WIN : HALF_FF] = self.z_in[3][:, 4 * WIN - HALF_FF :]
-        else:
-            total = self.z_in[0].astype(F32)
-            for q in range(1, 4):
-                total = total + self.z_in[q].astype(F32)
-            self.out[here, :] = total.astype(BF)
-        self.spread(self.second[0], self.at, 16, 4)
-
-    def spread(self, peers, start, size, stage):
-        block = self.out.at[self.rows(start, size), :]
-        for k, _, device in peers:
-            self.send(block, block, stage, k, dp=device)
-
-    def step5(self):
-        self.spread(self.first[0], self.at_first, self.first[2], 5)
-
-    def step6(self):
-        self.spread([(1, 0, self.sibling)], self.core * 128, 128, 6)
-
-    def step7(self):
-        pass
 
 
 def back_kernel(
@@ -705,7 +756,9 @@
     in2,
     mine,
     z_in,
+    ff_z,
     sem_flow,
+    sem_ff,
     sem_kv,
     sem_c,
     sem_in,
@@ -747,16 +800,19 @@
     flows = [
         GradSum(t, source, out, joined, wide_first, (r, d), buffers, sem_flow, go)
         for t, source, out, joined, wide_first in (
-            (0, ff_ref.at[0], ff_out.at[0], True, True),
-            (1, ff_ref.at[1], ff_out.at[1], True, False),
-            (2, ff_ref.at[2], ff_out.at[2], True, True),
-            (3, outw_grad, outw_out, False, False),
-            (4, proj_grad, proj_out, False, True),
+            (0, outw_grad, outw_out, False, True),
+            (1, proj_grad, proj_out, False, True),
         )
     ]
-    early, tail = flows[:4], flows[4]
-    for flow in early[:3]:
-        flow.step()
+    out, tail = flows
+    spare = (None,) * 6 + (ff_ref, ff_z)
+    ff = [
+        GradSum(t, None, ff_out.at[t], True, True, (r, d), spare, sem_ff, go)
+        for t in range(3)
+    ]
+    for flow in ff:
+        flow.cross_rows()
+        flow.done = 4
 
     def scatter(k, q):
         return go(
@@ -790,12 +846,12 @@
         grad_att += dot_nt(g_branch[j], outw_full[j])
     g_att[:, 448:512] = jnp.zeros((SHARE, 64), BF)
     g_att[:, 0:448] = grad_att.astype(BF)
-    for flow in early[:3]:
+    for flow in ff:
         flow.step()
     outw_grad[...] = jnp.zeros_like(outw_grad)
     for j in range(4):
         outw_grad[j, 0:FEAT, 0:448] = dot_tn(g_branch[j], att_ref[...]).astype(BF)
-    early[3].step()
+    out.step()
     query_at = lax.broadcasted_iota(jnp.int32, (SHARE, 1), 0) + MAXLEN
     key_at = lax.broadcasted_iota(jnp.int32, (SHARE, MAXLEN + SHARE), 1)
     mask[...] = jnp.where(
@@ -829,7 +885,9 @@
         else:
             dq[:, at : at + 128] = jnp.where(low, dq[:, at : at + 128], grad_q)
         if m == 1:
-            early[3].step()
+            out.step()
+            for flow in ff:
+                flow.step()
     wide_low = lax.broadcasted_iota(jnp.int32, (MAXLEN + SHARE, 128), 1) < 64
     dkv[...] = jnp.where(
         wide_low,
@@ -846,8 +904,7 @@
         )
         for i in (1, 2, 3, 4)
     ]
-    for flow in early:
-        flow.step()
+    out.step()
     total = dkv[MAXLEN : MAXLEN + SHARE, :].astype(F32)
     for i in (1, 2, 3, 4):
         kv_copies[i - 1].wait_recv()
@@ -875,8 +932,12 @@
     for j in range(4):
         small[j, 2:3, 0:512] = bias_a
         small[j, 2:3, 512:576] = bias_b
-    for flow in early:
+    out.step()
+    tail.step()
+    for flow in ff:
         flow.step()
+    tail.step()
+    out.step()
     tail.step()
 
     square = jnp.zeros((SHARE, 1), F32)
@@ -923,14 +984,12 @@
         return go(source, target, sem_s.at[0, stage, k - 1], sem_s.at[1, stage, k - 1], **device)
 
     copy = swap(0, small, small_in.at[0], 1, dp=sibling)
-    for flow in early:
-        flow.step()
+    out.step()
     tail.step()
     copy.wait_recv()
     small_x[0] = small[...] + small_in[0]
     copies = [swap(1, small_x.at[0], small_in.at[k], k, dp=p) for k, p in x_peers]
-    for flow in early:
-        flow.step()
+    out.step()
     tail.step()
     for copy in copies:
         copy.wait_recv()
@@ -941,16 +1000,13 @@
     small_x[2] = small_x[1] + small_in[4]
     copies = [swap(3, small_x.at[2, q], small_z.at[r], k, row=q) for k, q in row_peers]
     small_z[r] = small_x[2, r]
-    tail.step()
-    for flow in early:
-        flow.step()
     for copy in copies:
         copy.wait_recv()
     small_out[...] = small_z[0] + small_z[1] + small_z[2] + small_z[3]
     tail.step()
-    for flow in early:
+    out.step()
+    for flow in ff:
         flow.step()
-    tail.step()
     for copy in in_copies:
         copy.wait_recv()
     final.wait_recv()
@@ -964,7 +1020,7 @@
     shape = jax.ShapeDtypeStruct
     width = MAXLEN + SHARE
     blocked = pltpu.VMEM((4, SHARE, FEAT), BF)
-    count = 5
+    count = 2
     return vmem_call(
         back_kernel,
         17,
@@ -1008,7 +1064,9 @@
             pltpu.VMEM((count, 4, 48, WIN), BF),
             pltpu.VMEM((count, 4, 16, WIN), BF),
             pltpu.VMEM((count, 4, 16, WIN), BF),
+            pltpu.VMEM((3, 4, 16, WIN), BF),
             dma((2, count, 7, 3)),
+            dma((2, 3, 7, 3)),
             dma((2, 4)),
             dma((2,)),
             dma((2, 3)),
@@ -1062,7 +1120,7 @@
         cot_own,
         grad_second,
         out_partial,
-        ff_grads,
+        ff_part,
     ) = forward(
         activations,
         cotangent,
@@ -1093,7 +1151,7 @@
         cosine,
         sine,
         start_window,
-        ff_grads,
+        ff_part,
         out_partial,
     )
     width = project_weight.shape[1]

time: 247 us -> 250 us (1.012)
  the two profiles are of different devices: /device:TPU:1 before, /device:TPU:0 now
where the time goes in v1:
time: 250 us; the launch traced here: 247 us
  Pallas kernels  219 us (88%)
  local copies, waits for them, and re-layouts  18.6 us (7%)
  other arithmetic  7.65 us (3%)
    pallas_call x1, Pallas kernels, forward(): vmem_call(forward_kernel, 12, (shape((4, SHARE, FEAT), BF), shape((4, SHA...  127 us
    pallas_call x1, Pallas kernels, back(): vmem_call(back_kernel, 17, (shape((SHARD, FEAT), BF), shape((4, SHARE, FE...  92 us
    unnamed x12, local copies, waits for them, and re-layouts  9.85 us

profile of v1, /device:TPU:0, one launch (start us, length us, event | category | flops | bytes accessed | tf_op | source)
XLA Modules:
  0.0 246.6 jit_solution(15410568853973166798)
XLA Ops:
  0.6 0.0 copy-start
  0.7 0.8 broadcast_in_dim.11
  1.5 0.1 tile.14
  1.6 0.1 mul.41
  1.7 0.8 subtract_convert_fusion
  2.4 0.1 mul.38
  2.5 1.3 broadcast_in_dim.10.bias_ref
  3.8 1.3 select_maximum_fusion.gains_ref
  5.1 0.8 copy.31.start_ref
  5.9 1.2 fusion
  7.1 2.0 copy.28.act_ref
  9.1 2.0 copy.29.cot_ref
  11.2 0.0 copy-done
  11.2 1.5 copy.30.down_ref
  12.7 127.4 %shard_map.195 = (bf16[4,256,224]{2,1,0:T(8,128)(2,1)}, bf16[4,256,224]{2,1,0:T(8,128)(2,1)}, bf16[256,512]{1,0:T(8,128)(2,1)}, bf16[2,1280,128]{2,1,0:T(8,128)(...) custom-call(bf16[1024,224]{1,0:T(8,128)(2,1)} %copy.28.act_ref, ...), custom_call_target="tpu_custom_call" | custom-call | tf_op jit(solution)/shard_map/pallas_call | solution.py:644
  140.1 92.0 %shard_map.196 = (bf16[1024,224]{1,0:T(8,128)(2,1)}, bf16[4,256,224]{2,1,0:T(8,128)(2,1)}, bf16[3,256,2432]{2,1,0:T(8,128)(2,1)}, bf16[256,640]{1,0:T(8,128)(2,1...) custom-call(f32[4,256,224]{2,1,0:T(8,128)} %get-tuple-element.30.second_ref, f32[4,256,224]{2,1,0:T(8,128)} %get-tuple-element.31.mid_ref, ...), custom_call_target="tpu_custom_call" | custom-call | tf_op jit(solution)/shard_map/pallas_call | solution.py:1024
  232.1 0.0 copy-start.2
  232.1 0.0 copy-start.1
  232.1 2.1 copy.33
  234.2 1.3 fusion.1
  235.6 1.3 slice_reduce_fusion
  236.9 1.0 convert_bitcast_fusion
  237.9 1.0 copy.35
  238.8 0.0 copy-done.2
  238.8 0.8 slice_convert_fusion.1
  239.7 0.0 copy-done.1
  239.7 0.1 bitcast_convert_fusion
  239.8 1.3 copy.34
  241.1 2.4 slice_convert_fusion
  243.5 2.9 %slice_bitcast_fusion = (f32[2432,224]{0,1:T(8,128)}, f32[224,2432]{1,0:T(8,128)}, f32[224,2432]{1,0:T(8,128)}) fusion(f32[3,224,2432]{2,1,0:T(8,128)S(1)} %slice_convert_fusion), kind=kLoop, calls=%fused_computation.1 | loop fusion | bytes 13074432 | tf_op jit(solution)/shard_map/transpose | solution.py:1169
  (3 shorter events, 0.0 us)
Async XLA Ops:
  0.6 10.5 %copy-start = (bf16[2432,224]{0,1:T(8,128)(2,1)S(1)}, bf16[2432,224]{0,1:T(8,128)(2,1)}, u32[]{:S(2)}) copy-start(bf16[2432,224]{0,1:T(8,128)(2,1)} %param.21) | copy-start | bytes 3268612
  232.1 6.7 %copy-start.2 = (bf16[256,640]{1,0:T(8,128)(2,1)S(1)}, bf16[256,640]{1,0:T(8,128)(2,1)}, u32[]{:S(2)}) copy-start(bf16[256,640]{1,0:T(8,128)(2,1)} %get-tuple-element.47) | copy-start | bytes 983044
  232.1 7.6 %copy-start.1 = (bf16[4,256,224]{2,1,0:T(8,128)(2,1)S(1)}, bf16[4,256,224]{2,1,0:T(8,128)(2,1)}, u32[]{:S(2)}) copy-start(bf16[4,256,224]{2,1,0:T(8,128)(2,1)} %get-tuple-element.45) | copy-start | bytes 1376260

commit v2 on v1

--- a/solution.py
+++ b/solution.py
@@ -886,8 +886,7 @@
             dq[:, at : at + 128] = jnp.where(low, dq[:, at : at + 128], grad_q)
         if m == 1:
             out.step()
-            for flow in ff:
-                flow.step()
+            ff[0].step()
     wide_low = lax.broadcasted_iota(jnp.int32, (MAXLEN + SHARE, 128), 1) < 64
     dkv[...] = jnp.where(
         wide_low,
@@ -934,8 +933,8 @@
         small[j, 2:3, 512:576] = bias_b
     out.step()
     tail.step()
-    for flow in ff:
-        flow.step()
+    ff[1].step()
+    ff[2].step()
     tail.step()
     out.step()
     tail.step()
@@ -986,6 +985,7 @@
     copy = swap(0, small, small_in.at[0], 1, dp=sibling)
     out.step()
     tail.step()
+    ff[0].step()
     copy.wait_recv()
     small_x[0] = small[...] + small_in[0]
     copies = [swap(1, small_x.at[0], small_in.at[k], k, dp=p) for k, p in x_peers]
@@ -1000,6 +1000,8 @@
     small_x[2] = small_x[1] + small_in[4]
     copies = [swap(3, small_x.at[2, q], small_z.at[r], k, row=q) for k, q in row_peers]
     small_z[r] = small_x[2, r]
+    ff[1].step()
+    ff[2].step()
     for copy in copies:
         copy.wait_recv()
     small_out[...] = small_z[0] + small_z[1] + small_z[2] + small_z[3]

time: 250 us -> 238 us (0.952)
  the two profiles are of different devices: /device:TPU:0 before, /device:TPU:1 now
where the time goes in v2:
time: 238 us; the launch traced here: 235 us
  Pallas kernels  208 us (87%)
  local copies, waits for them, and re-layouts  18.6 us (8%)
  other arithmetic  7.65 us (3%)
    pallas_call x1, Pallas kernels, forward(): vmem_call(forward_kernel, 12, (shape((4, SHARE, FEAT), BF), shape((4, SHA...  128 us
    pallas_call x1, Pallas kernels, back(): vmem_call(back_kernel, 17, (shape((SHARD, FEAT), BF), shape((4, SHARE, FE...  79.9 us
    unnamed x12, local copies, waits for them, and re-layouts  9.85 us

profile of v2, /device:TPU:1, one launch (start us, length us, event | category | flops | bytes accessed | tf_op | source)
XLA Modules:
  0.0 234.8 jit_solution(16266703188048554252)
XLA Ops:
  0.6 0.0 copy-start
  0.7 0.8 broadcast_in_dim.11
  1.5 0.1 tile.14
  1.6 0.1 mul.41
  1.7 0.8 subtract_convert_fusion
  2.4 0.1 mul.38
  2.5 1.3 broadcast_in_dim.10.bias_ref
  3.8 1.3 select_maximum_fusion.gains_ref
  5.1 0.8 copy.31.start_ref
  5.9 1.2 fusion
  7.1 2.0 copy.28.act_ref
  9.1 2.0 copy.29.cot_ref
  11.2 0.0 copy-done
  11.2 1.5 copy.30.down_ref
  12.7 127.7 %shard_map.195 = (bf16[4,256,224]{2,1,0:T(8,128)(2,1)}, bf16[4,256,224]{2,1,0:T(8,128)(2,1)}, bf16[256,512]{1,0:T(8,128)(2,1)}, bf16[2,1280,128]{2,1,0:T(8,128)(...) custom-call(bf16[1024,224]{1,0:T(8,128)(2,1)} %copy.28.act_ref, ...), custom_call_target="tpu_custom_call" | custom-call | tf_op jit(solution)/shard_map/pallas_call | solution.py:644
  140.4 79.9 %shard_map.196 = (bf16[1024,224]{1,0:T(8,128)(2,1)}, bf16[4,256,224]{2,1,0:T(8,128)(2,1)}, bf16[3,256,2432]{2,1,0:T(8,128)(2,1)}, bf16[256,640]{1,0:T(8,128)(2,1...) custom-call(f32[4,256,224]{2,1,0:T(8,128)} %get-tuple-element.30.second_ref, f32[4,256,224]{2,1,0:T(8,128)} %get-tuple-element.31.mid_ref, ...), custom_call_target="tpu_custom_call" | custom-call | tf_op jit(solution)/shard_map/pallas_call | solution.py:1026
  220.3 0.0 copy-start.2
  220.3 0.0 copy-start.1
  220.3 2.1 copy.33
  222.4 1.3 fusion.1
  223.8 1.3 slice_reduce_fusion
  225.1 1.0 convert_bitcast_fusion
  226.1 1.0 copy.35
  227.0 0.0 copy-done.2
  227.0 0.8 slice_convert_fusion.1
  227.9 0.0 copy-done.1
  227.9 0.1 bitcast_convert_fusion
  228.0 1.3 copy.34
  229.2 2.4 %slice_convert_fusion = f32[3,224,2432]{2,1,0:T(8,128)S(1)} fusion(bf16[3,256,2432]{2,1,0:T(8,128)(2,1)} %get-tuple-element.49), kind=kLoop, calls=%fused_computation | loop fusion | flops 1634304 | bytes 9805824 | tf_op jit(solution)/shard_map/convert_element_type | solution.py:1160
  231.7 2.9 %slice_bitcast_fusion = (f32[2432,224]{0,1:T(8,128)}, f32[224,2432]{1,0:T(8,128)}, f32[224,2432]{1,0:T(8,128)}) fusion(f32[3,224,2432]{2,1,0:T(8,128)S(1)} %slice_convert_fusion), kind=kLoop, calls=%fused_computation.1 | loop fusion | bytes 13074432 | tf_op jit(solution)/shard_map/transpose | solution.py:1171
  (3 shorter events, 0.0 us)
Async XLA Ops:
  0.6 10.5 %copy-start = (bf16[2432,224]{0,1:T(8,128)(2,1)S(1)}, bf16[2432,224]{0,1:T(8,128)(2,1)}, u32[]{:S(2)}) copy-start(bf16[2432,224]{0,1:T(8,128)(2,1)} %param.21) | copy-start | bytes 3268612
  220.3 6.7 %copy-start.2 = (bf16[256,640]{1,0:T(8,128)(2,1)S(1)}, bf16[256,640]{1,0:T(8,128)(2,1)}, u32[]{:S(2)}) copy-start(bf16[256,640]{1,0:T(8,128)(2,1)} %get-tuple-element.47) | copy-start | bytes 983044
  220.3 7.6 %copy-start.1 = (bf16[4,256,224]{2,1,0:T(8,128)(2,1)S(1)}, bf16[4,256,224]{2,1,0:T(8,128)(2,1)}, u32[]{:S(2)}) copy-start(bf16[4,256,224]{2,1,0:T(8,128)(2,1)} %get-tuple-element.45) | copy-start | bytes 1376260

commit v3 on v2

--- a/solution.py
+++ b/solution.py
@@ -245,6 +245,7 @@
     cot_all,
     mask,
     own_kv,
+    kv_pack,
     c_send,
     c_in,
     second_in,
@@ -451,31 +452,38 @@
     tile = turned[:, 384:512]
     lane = lax.broadcasted_iota(jnp.int32, (SHARE, 128), 1)
     low = lane < 64
-    own_kv[0] = jnp.where(low, pltpu.roll(tile, 64, 1), tile).astype(BF)
     double = (
         lax.rem(lax.broadcasted_iota(jnp.int32, (64, 128), 1), 64)
         == lax.broadcasted_iota(jnp.int32, (64, 128), 0)
     ).astype(F32).astype(BF)
-    own_kv[1] = dot(values, double).astype(BF)
+    own_kv[...] = jnp.where(low, pltpu.roll(tile, 64, 1), dot(values, double)).astype(BF)
     kv_copies = [
         go(
             own_kv,
-            kv_out.at[:, (4 - i) * SHARE : (5 - i) * SHARE, :],
+            kv_pack.at[(4 - i) * SHARE : (5 - i) * SHARE, :],
             sem_kv.at[0, i - 1],
             sem_kv.at[1, i - 1],
             **near(i),
         )
         for i in (1, 2, 3, 4)
     ]
-    kv_out[:, MAXLEN : MAXLEN + SHARE, :] = own_kv[...]
+    kv_pack[MAXLEN : MAXLEN + SHARE, :] = own_kv[...]
     for w in (2, 3, 4):
         pass_on(w, fetched[w])
     for copy in kv_copies:
         copy.wait_recv()
-    cot_copies = [
-        go(cot_ref, cot_all.at[r], sem_cot.at[0, k - 1], sem_cot.at[1, k - 1], row=q)
-        for k, q in (peers[0], peers[2], peers[1])
-    ]
+    right, across, left = [q for _, q in peers]
+
+    def cot_go(source, target, index, q):
+        return go(source, target, sem_cot.at[0, index], sem_cot.at[1, index], row=q)
+
+    cot_left = cot_go(cot_ref, cot_all.at[r], 0, right)
+    cot_right = cot_go(cot_ref, cot_all.at[r], 1, left)
+    packed = kv_pack[...].astype(F32)
+    turned_pack = pltpu.roll(packed, 64, 1)
+    first_half = lax.broadcasted_iota(jnp.int32, packed.shape, 1) < 64
+    kv_out[0] = jnp.where(first_half, packed, turned_pack).astype(BF)
+    kv_out[1] = jnp.where(first_half, turned_pack, packed).astype(BF)
     for m in range(HEADS // GROUPS):
         at = 128 * (m // 2)
         mine = low if m % 2 == 0 else jnp.logical_not(low)
@@ -499,6 +507,12 @@
         c_send[j] = dot(att_out[...], outw_full[j]).astype(BF)
     cross = rcopy(c_send, c_in, sem_c.at[0], sem_c.at[1], col=1 - c)
     cross.start()
+    cot_left.wait_recv()
+    upper = cot_all.at[left, 0 : SHARD // 2, :]
+    cot_copies = [cot_go(upper, upper, 2, right)]
+    cot_right.wait_recv()
+    lower = cot_all.at[right, SHARD // 2 : SHARD, :]
+    cot_copies.append(cot_go(lower, lower, 3, left))
     for w in (2, 3, 4):
         shared[w] = share(w, fetched[w])
     cross.wait_recv()
@@ -512,8 +526,6 @@
     rate = lax.rsqrt(square / D + EPS)
     for j in range(4):
         ns_all[j, span(r), :] = (mid_out[j] * rate * gains_full[j, 1:2, :]).astype(BF)
-
-    right, across, left = [q for _, q in peers]
 
     def spread(blocks, source, index, q):
         part = ns_all.at[blocks, span(source), :]
@@ -666,7 +678,8 @@
             pltpu.VMEM((4, WIN, FEAT), BF),
             pltpu.VMEM((4, SHARD, FEAT), BF),
             pltpu.VMEM((SHARE, width), F32),
-            pltpu.VMEM((2, SHARE, 128), BF),
+            pltpu.VMEM((SHARE, 128), BF),
+            pltpu.VMEM((width, 128), BF),
             blocked,
             blocked,
             blocked,
@@ -688,7 +701,7 @@
             dma((2, 5, 3)),
             dma((2, 3, 3, 3)),
             dma((2, 5)),
-            dma((2, 3)),
+            dma((2, 4)),
             dma((2, 4)),
             dma((2,)),
             dma((2, 4)),

time: 238 us -> 234 us (0.983)
  Pallas kernels: 208 us -> 203 us
where the time goes in v3:
time: 234 us; the launch traced here: 230 us
  Pallas kernels  203 us (87%)
  local copies, waits for them, and re-layouts  18.6 us (8%)
  other arithmetic  7.65 us (3%)
    pallas_call x1, Pallas kernels, forward(): vmem_call(forward_kernel, 12, (shape((4, SHARE, FEAT), BF), shape((4, SHA...  126 us
    pallas_call x1, Pallas kernels, back(): vmem_call(back_kernel, 17, (shape((SHARD, FEAT), BF), shape((4, SHARE, FE...  77.6 us
    unnamed x12, local copies, waits for them, and re-layouts  9.85 us

profile of v3, /device:TPU:1, one launch (start us, length us, event | category | flops | bytes accessed | tf_op | source)
XLA Modules:
  0.0 230.3 jit_solution(12344476409829372965)
XLA Ops:
  0.6 0.0 copy-start
  0.7 0.8 broadcast_in_dim.11
  1.5 0.1 tile.14
  1.6 0.1 mul.41
  1.7 0.8 subtract_convert_fusion
  2.4 0.1 mul.38
  2.5 1.3 broadcast_in_dim.10.bias_ref
  3.8 1.3 select_maximum_fusion.gains_ref
  5.1 0.8 copy.31.start_ref
  5.9 1.2 fusion
  7.1 2.0 copy.28.act_ref
  9.1 2.0 copy.29.cot_ref
  11.2 0.0 copy-done
  11.2 1.5 copy.30.down_ref
  12.7 125.5 %shard_map.195 = (bf16[4,256,224]{2,1,0:T(8,128)(2,1)}, bf16[4,256,224]{2,1,0:T(8,128)(2,1)}, bf16[256,512]{1,0:T(8,128)(2,1)}, bf16[2,1280,128]{2,1,0:T(8,128)(...) custom-call(bf16[1024,224]{1,0:T(8,128)(2,1)} %copy.28.act_ref, ...), custom_call_target="tpu_custom_call" | custom-call | tf_op jit(solution)/shard_map/pallas_call | solution.py:656
  138.2 77.6 %shard_map.196 = (bf16[1024,224]{1,0:T(8,128)(2,1)}, bf16[4,256,224]{2,1,0:T(8,128)(2,1)}, bf16[3,256,2432]{2,1,0:T(8,128)(2,1)}, bf16[256,640]{1,0:T(8,128)(2,1...) custom-call(f32[4,256,224]{2,1,0:T(8,128)} %get-tuple-element.30.second_ref, f32[4,256,224]{2,1,0:T(8,128)} %get-tuple-element.31.mid_ref, ...), custom_call_target="tpu_custom_call" | custom-call | tf_op jit(solution)/shard_map/pallas_call | solution.py:1039
  215.8 0.0 copy-start.2
  215.8 0.0 copy-start.1
  215.8 2.1 copy.33
  217.9 1.3 fusion.1
  219.3 1.3 slice_reduce_fusion
  220.6 1.0 convert_bitcast_fusion
  221.6 1.0 copy.35
  222.5 0.0 copy-done.2
  222.5 0.8 slice_convert_fusion.1
  223.4 0.0 copy-done.1
  223.4 0.1 bitcast_convert_fusion
  223.5 1.3 copy.34
  224.8 2.4 %slice_convert_fusion = f32[3,224,2432]{2,1,0:T(8,128)S(1)} fusion(bf16[3,256,2432]{2,1,0:T(8,128)(2,1)} %get-tuple-element.49), kind=kLoop, calls=%fused_computation | loop fusion | flops 1634304 | bytes 9805824 | tf_op jit(solution)/shard_map/convert_element_type | solution.py:1173
  227.2 2.9 %slice_bitcast_fusion = (f32[2432,224]{0,1:T(8,128)}, f32[224,2432]{1,0:T(8,128)}, f32[224,2432]{1,0:T(8,128)}) fusion(f32[3,224,2432]{2,1,0:T(8,128)S(1)} %slice_convert_fusion), kind=kLoop, calls=%fused_computation.1 | loop fusion | bytes 13074432 | tf_op jit(solution)/shard_map/transpose | solution.py:1184
  (3 shorter events, 0.0 us)
Async XLA Ops:
  0.6 10.5 %copy-start = (bf16[2432,224]{0,1:T(8,128)(2,1)S(1)}, bf16[2432,224]{0,1:T(8,128)(2,1)}, u32[]{:S(2)}) copy-start(bf16[2432,224]{0,1:T(8,128)(2,1)} %param.21) | copy-start | bytes 3268612
  215.8 6.7 %copy-start.2 = (bf16[256,640]{1,0:T(8,128)(2,1)S(1)}, bf16[256,640]{1,0:T(8,128)(2,1)}, u32[]{:S(2)}) copy-start(bf16[256,640]{1,0:T(8,128)(2,1)} %get-tuple-element.47) | copy-start | bytes 983044
  215.8 7.6 %copy-start.1 = (bf16[4,256,224]{2,1,0:T(8,128)(2,1)S(1)}, bf16[4,256,224]{2,1,0:T(8,128)(2,1)}, u32[]{:S(2)}) copy-start(bf16[4,256,224]{2,1,0:T(8,128)(2,1)} %get-tuple-element.45) | copy-start | bytes 1376260

commit v4 on v3

--- a/solution.py
+++ b/solution.py
@@ -238,6 +238,7 @@
     cot_out,
     second_out,
     op_out,
+    down_out,
     mine_out,
     gate_full,
     up_full,
@@ -602,16 +603,17 @@
     buffers = (core_in, part, low_buf, in1, low2, in2, mine_out, None)
     flows = [
         GradSum(t, grads.at[t], None, True, True, (r, d), buffers, sem_flow, go)
-        for t in range(3)
+        for t in range(2)
     ]
-    grads[:, :, FEAT:PADF, :] = jnp.zeros((3, 4, PADF - FEAT, WIN), BF)
-    for t, left_side, right_side in ((0, ns_all, gg), (1, ns_all, gu), (2, cot_all, hid)):
+    grads[:, :, FEAT:PADF, :] = jnp.zeros((2, 4, PADF - FEAT, WIN), BF)
+    down_out[:, FEAT:PADF, :] = jnp.zeros((4, PADF - FEAT, WIN), BF)
+    for t, right_side in ((0, gg), (1, gu)):
         for j in range(4):
-            grads[t, j, 0:FEAT, :] = dot_tn(left_side[j], right_side[...]).astype(BF)
+            grads[t, j, 0:FEAT, :] = dot_tn(ns_all[j], right_side[...]).astype(BF)
         flows[t].step()
         if t:
             flows[t - 1].step()
-    flows[2].step()
+    flows[1].step()
     cross.wait_send()
     crosses = []
     for h in (0, 2):
@@ -629,6 +631,9 @@
                 col=1 - c,
             )
         )
+        if h == 0:
+            for j in range(4):
+                down_out[j, 0:FEAT, :] = dot_tn(cot_all[j], hid[...]).astype(BF)
     for j in range(4):
         for q in range(4):
             op_out[j, q * SHARE : (q + 1) * SHARE, :] = dot(
@@ -670,7 +675,8 @@
             shape((4, SHARE, FEAT), BF),
             shape((4, SHARE, FEAT), F32),
             shape((4, SHARD, FEAT), BF),
-            shape((3, 4, 16, WIN), BF),
+            shape((4, PADF, WIN), BF),
+            shape((2, 4, 16, WIN), BF),
         ),
         [
             pltpu.VMEM((4, FEAT, WIN), BF),
@@ -689,7 +695,7 @@
             pltpu.VMEM((SHARD, WIN), BF),
             pltpu.VMEM((4, 4, SHARE, FEAT), BF),
             pltpu.VMEM((3, 4, SHARE, FEAT), BF),
-            pltpu.VMEM((3, 4, PADF, WIN), BF),
+            pltpu.VMEM((2, 4, PADF, WIN), BF),
             pltpu.VMEM((3, 4, 128, WIN), BF),
             pltpu.VMEM((3, 4, 128, WIN), F32),
             pltpu.VMEM((3, 4, 128, WIN), BF),
@@ -732,6 +738,7 @@
     start_ref,
     ff_ref,
     op_ref,
+    down_ref,
     block_out,
     input_out,
     ff_out,
@@ -815,17 +822,20 @@
         for t, source, out, joined, wide_first in (
             (0, outw_grad, outw_out, False, True),
             (1, proj_grad, proj_out, False, True),
+            (2, down_ref, ff_out.at[2], True, True),
         )
     ]
-    out, tail = flows
+    out, tail, down = flows
+    down.step()
     spare = (None,) * 6 + (ff_ref, ff_z)
     ff = [
         GradSum(t, None, ff_out.at[t], True, True, (r, d), spare, sem_ff, go)
-        for t in range(3)
+        for t in range(2)
     ]
     for flow in ff:
         flow.cross_rows()
         flow.done = 4
+    ff.append(down)
 
     def scatter(k, q):
         return go(
@@ -899,6 +909,7 @@
             dq[:, at : at + 128] = jnp.where(low, dq[:, at : at + 128], grad_q)
         if m == 1:
             out.step()
+            down.step()
             ff[0].step()
     wide_low = lax.broadcasted_iota(jnp.int32, (MAXLEN + SHARE, 128), 1) < 64
     dkv[...] = jnp.where(
@@ -917,11 +928,13 @@
         for i in (1, 2, 3, 4)
     ]
     out.step()
+    down.step()
     total = dkv[MAXLEN : MAXLEN + SHARE, :].astype(F32)
     for i in (1, 2, 3, 4):
         kv_copies[i - 1].wait_recv()
         total += dkv_in[i - 1].astype(F32)
     op_copies.append(scatter(*row_peers[1]))
+    down.step()
     turned = pltpu.roll(total, 64, 1)
     dq[:, 384:512] = jnp.where(low, dq[:, 384:512], turned)
     gv[...] = turned[:, 0:64].astype(BF)
@@ -1035,10 +1048,10 @@
     shape = jax.ShapeDtypeStruct
     width = MAXLEN + SHARE
     blocked = pltpu.VMEM((4, SHARE, FEAT), BF)
-    count = 2
+    count = 3
     return vmem_call(
         back_kernel,
-        17,
+        18,
         (
             shape((SHARD, FEAT), BF),
             shape((4, SHARE, FEAT), BF),
@@ -1135,6 +1148,7 @@
         cot_own,
         grad_second,
         out_partial,
+        down_part,
         ff_part,
     ) = forward(
         activations,
@@ -1168,6 +1182,7 @@
         start_window,
         ff_part,
         out_partial,
+        down_part,
     )
     width = project_weight.shape[1]
     ff_sum = ff_sum[:, :FEAT].astype(F32)

time: 234 us -> 237 us (1.013)
  Pallas kernels: 203 us -> 206 us
    pallas_call x1, Pallas kernels: 77.6 us -> 87.5 us  [back(): vmem_call(back_kernel, 18, (shape((SHARD, FEAT), BF), shape((4, SHARE, FE...]
    pallas_call x1, Pallas kernels: 126 us -> 119 us  [forward(): vmem_call(forward_kernel, 12, (shape((4, SHARE, FEAT), BF), shape((4, SHA...]
where the time goes in v4:
time: 237 us; the launch traced here: 233 us
  Pallas kernels  206 us (87%)
  local copies, waits for them, and re-layouts  18.6 us (8%)
  other arithmetic  7.65 us (3%)
    pallas_call x1, Pallas kernels, forward(): vmem_call(forward_kernel, 12, (shape((4, SHARE, FEAT), BF), shape((4, SHA...  119 us
    pallas_call x1, Pallas kernels, back(): vmem_call(back_kernel, 18, (shape((SHARD, FEAT), BF), shape((4, SHARE, FE...  87.5 us
    unnamed x12, local copies, waits for them, and re-layouts  9.85 us

profile of v4, /device:TPU:1, one launch (start us, length us, event | category | flops | bytes accessed | tf_op | source)
XLA Modules:
  0.0 233.3 jit_solution(16912032914590571885)
XLA Ops:
  0.6 0.0 copy-start
  0.7 0.8 broadcast_in_dim.11
  1.5 0.1 tile.14
  1.6 0.1 mul.41
  1.7 0.8 subtract_convert_fusion
  2.4 0.1 mul.38
  2.5 1.3 broadcast_in_dim.10.bias_ref
  3.8 1.3 select_maximum_fusion.gains_ref
  5.1 0.8 copy.31.start_ref
  5.9 1.2 fusion
  7.1 2.0 copy.28.act_ref
  9.1 2.0 copy.29.cot_ref
  11.2 0.0 copy-done
  11.2 1.5 copy.30.down_ref
  12.7 118.6 %shard_map.195 = (bf16[4,256,224]{2,1,0:T(8,128)(2,1)}, bf16[4,256,224]{2,1,0:T(8,128)(2,1)}, bf16[256,512]{1,0:T(8,128)(2,1)}, bf16[2,1280,128]{2,1,0:T(8,128)(...) custom-call(bf16[1024,224]{1,0:T(8,128)(2,1)} %copy.28.act_ref, ...), custom_call_target="tpu_custom_call" | custom-call | tf_op jit(solution)/shard_map/pallas_call | solution.py:661
  131.3 87.5 %shard_map.196 = (bf16[1024,224]{1,0:T(8,128)(2,1)}, bf16[4,256,224]{2,1,0:T(8,128)(2,1)}, bf16[3,256,2432]{2,1,0:T(8,128)(2,1)}, bf16[256,640]{1,0:T(8,128)(2,1...) custom-call(f32[4,256,224]{2,1,0:T(8,128)} %get-tuple-element.31.second_ref, f32[4,256,224]{2,1,0:T(8,128)} %get-tuple-element.32.mid_ref, ...), custom_call_target="tpu_custom_call" | custom-call | tf_op jit(solution)/shard_map/pallas_call | solution.py:1052
  218.8 0.0 copy-start.2
  218.8 0.0 copy-start.1
  218.8 2.1 copy.33
  220.9 1.3 fusion.1
  222.2 1.3 slice_reduce_fusion
  223.6 1.0 convert_bitcast_fusion
  224.6 1.0 copy.35
  225.5 0.0 copy-done.2
  225.5 0.8 slice_convert_fusion.1
  226.4 0.0 copy-done.1
  226.4 0.1 bitcast_convert_fusion
  226.5 1.3 copy.34
  227.7 2.4 %slice_convert_fusion = f32[3,224,2432]{2,1,0:T(8,128)S(1)} fusion(bf16[3,256,2432]{2,1,0:T(8,128)(2,1)} %get-tuple-element.51), kind=kLoop, calls=%fused_computation | loop fusion | flops 1634304 | bytes 9805824 | tf_op jit(solution)/shard_map/convert_element_type | solution.py:1188
  230.2 2.9 %slice_bitcast_fusion = (f32[2432,224]{0,1:T(8,128)}, f32[224,2432]{1,0:T(8,128)}, f32[224,2432]{1,0:T(8,128)}) fusion(f32[3,224,2432]{2,1,0:T(8,128)S(1)} %slice_convert_fusion), kind=kLoop, calls=%fused_computation.1 | loop fusion | bytes 13074432 | tf_op jit(solution)/shard_map/transpose | solution.py:1199
  (3 shorter events, 0.0 us)
Async XLA Ops:
  0.6 10.5 %copy-start = (bf16[2432,224]{0,1:T(8,128)(2,1)S(1)}, bf16[2432,224]{0,1:T(8,128)(2,1)}, u32[]{:S(2)}) copy-start(bf16[2432,224]{0,1:T(8,128)(2,1)} %param.21) | copy-start | bytes 3268612
  218.8 6.7 %copy-start.2 = (bf16[256,640]{1,0:T(8,128)(2,1)S(1)}, bf16[256,640]{1,0:T(8,128)(2,1)}, u32[]{:S(2)}) copy-start(bf16[256,640]{1,0:T(8,128)(2,1)} %get-tuple-element.49) | copy-start | bytes 983044
  218.8 7.6 %copy-start.1 = (bf16[4,256,224]{2,1,0:T(8,128)(2,1)S(1)}, bf16[4,256,224]{2,1,0:T(8,128)(2,1)}, u32[]{:S(2)}) copy-start(bf16[4,256,224]{2,1,0:T(8,128)(2,1)} %get-tuple-element.47) | copy-start | bytes 1376260
